TPU v7x, 256 devices: a whole 4x4x8 slice. The times are simulated.
256 devices in a mesh: aux: 32 (over y, z), occ: 8 (over x, core).
Axes of the slice: x: 4, y: 4, z: 8, core: 2. Of those that a mesh axis runs over, the one named last changes fastest.
Arguments:
- three_index: bfloat16 [32, 2048, 128, 128], P('occ', 'aux'), may hold values from -6 to 6
- occ_coeff: bfloat16 [1024, 256], replicated, may hold values from -0.375 to 0.375
- occ_mask: int32 [8, 8], replicated, may hold values 0 or 1
- screen_list: int32 [32, 32], P('aux', 'occ'), may hold values from 0 to 7, as said below
- screen_count: int32 [32, 8], P('aux', 'occ'), may hold values from 1 to 4, as said below
- owner_order: int32 [64], replicated, may hold values from 0 to 63, each once
Outputs:
- exchange: float32 [64, 128, 128], P('aux', 'occ')
Inputs may be any that keep to these rules, and one draw needn't show every extreme that they name: `screen_list`: the 4 entries of one aux index and one first-index block are distinct basis blocks. `screen_count`: slots below the count are live; in every aux index some first-index block has all 4 slots live.
All inputs are finite; a program needn't handle non-finite values.
Results may differ from a plain program's by a relative error of at most 0.0003.
Values may be sent and summed in bfloat16 or wider, within the bound.
A program may use at most 64 MiB of HBM per device.

v0:
```python
import math

import jax
import jax.numpy as jnp
from jax import lax
from jax.sharding import PartitionSpec as P


def shards(three_index, occ_coeff, occ_mask, screen_list, screen_count, owner_order):
    occ_groups = lax.axis_size("occ")
    aux_groups = lax.axis_size("aux")
    own_index = lax.axis_index("occ")
    slot_total, aux_rows, block_size, _ = three_index.shape
    orbitals = occ_coeff.shape[1]
    orb_block = orbitals // occ_groups
    block_count = occ_mask.shape[0]
    pair_total = owner_order.shape[0]
    col_mask = jnp.repeat(occ_mask, orb_block, axis=1).astype(jnp.bfloat16)
    masked_coeff = occ_coeff.reshape(block_count, block_size, orbitals) * col_mask[:, None, :]
    listed = screen_list[0]
    live_count = screen_count[0, 0]

    def add_slot(slot, accum):
        column = lax.dynamic_index_in_dim(masked_coeff, listed[slot], 0, keepdims=False)
        integrals = lax.dynamic_index_in_dim(three_index, slot, 0, keepdims=False)
        return accum + lax.dot_general(
            column, integrals, (((0,), (2,)), ((), ())), preferred_element_type=jnp.float32
        )

    empty = jnp.zeros((orbitals, aux_rows, block_size), jnp.float32)
    accum = lax.fori_loop(0, live_count, add_slot, empty)
    own_row = lax.dynamic_index_in_dim(occ_mask, own_index, 0, keepdims=False)
    row_mask = jnp.repeat(own_row, orb_block).astype(jnp.float32)
    halfway = (accum * row_mask[:, None, None]).astype(jnp.bfloat16)
    received = lax.all_to_all(
        halfway.reshape(occ_groups, orb_block, aux_rows, block_size),
        "occ",
        split_axis=0,
        concat_axis=0,
        tiled=True,
    )
    flat = received.reshape(block_count, orb_block * aux_rows, block_size)
    dense = lax.dot_general(
        flat, flat, (((1,), (1,)), ((), ())), preferred_element_type=jnp.float32
    )
    scale = 1.0 / math.sqrt(aux_rows * aux_groups * orbitals)
    blocks = dense.transpose(0, 2, 1, 3).reshape(pair_total, block_size, block_size) * scale
    ordered = jnp.take(blocks, owner_order, axis=0)
    shares = lax.psum_scatter(ordered, "aux", scatter_dimension=0, tiled=True)
    result = lax.psum_scatter(shares, "occ", scatter_dimension=1, tiled=True)
    return result


def solution(mesh):
    in_specs = (P("occ", "aux", None, None), P(), P(), P("aux", "occ"), P("aux", "occ"), P())
    out_specs = P("aux", "occ", None)
    return jax.shard_map(shards, mesh=mesh, in_specs=in_specs, out_specs=out_specs, check_vma=False)
```

profile of v0, /device:TPU:1, one launch (start us, length us, event | category | flops | bytes accessed | tf_op | source)
XLA Modules:
  0.0 405.5 jit_solution(7439338267059523445)
XLA Ops:
  6.5 0.7 convert_element_type.28
  7.2 0.1 broadcast_in_dim.25
  7.3 0.1 convert_element_type.29
  7.4 1.1 broadcast_multiply_fusion
  8.5 0.0 copy-start
  8.5 4.3 %broadcast_in_dim.24 = f32[256,64,128]{2,0,1:T(8,128)} broadcast(f32[]{:T(128)} %constant.40.clone.1), dimensions={} | broadcast | bytes 8388612 | tf_op jit(solution)/shard_map/broadcast_in_dim | solution.py:30
  12.8 0.0 copy-done
  12.8 12.4 %while.10 = (s32[]{:T(128)}, f32[256,64,128]{2,0,1:T(8,128)}, s32[]{:T(128)}, s32[4]{0:T(128)S(1)}, bf16[8,128,256]{2,1,0:T(8,128)(2,1)S(1)}, /*index=5*/bf16[4,...) while((s32[]{:T(128)}, f32[256,64,128]{2,0,1:T(8,128)}, s32[]{:T(128)}, ...), condition=%wide.region_1.2_spmd, body=%wide.region_0.1_spmd.sunk | while | flops 538968064 | bytes 18940100 | solution.py:31
  13.4 0.6 dynamic_slice.30
  15.9 8.5 %convolution_add_fusion.2 = f32[256,64,128]{2,0,1:T(8,128)} fusion(f32[256,64,128]{2,0,1:T(8,128)} %get-tuple-element.106, bf16[4,64,128,128]{3,2,1,0:T(8,128)(2,1)} %get-tuple-element.120, s32[]{:T(128)S(6)} %select_n.31, bf16[8,128,256]{2,1,0:T(8,128)(2,1)S(1)} %get-tuple-element.119, s32[]{:T(128)S(6)} %select_n.32), kind=kOutput, calls=%fused_computation.1.clone.1 | convolution fusion | flops 538968064 | bytes 18939912 | tf_op jit(solution)/shard_map/while/body/dot_general | solution.py:26
  25.1 0.7 convert_bitcast_fusion
  25.8 0.1 broadcast_in_dim.26
  25.9 0.1 convert_element_type.32
  26.0 4.5 %multiply_convert_fusion = bf16[256,64,128]{2,0,1:T(8,128)(2,1)S(1)} fusion(f32[256,64,128]{2,0,1:T(8,128)} %get-tuple-element.38, f32[256]{0:T(256)S(1)} %convert_element_type.32), kind=kLoop, calls=%fused_computation.7 | loop fusion | flops 4194304 | bytes 12583936 | tf_op jit(solution)/shard_map/convert_element_type | solution.py:34
  30.5 4.7 %copy.9 = bf16[256,64,128]{2,1,0:T(8,128)(2,1)} copy(bf16[256,64,128]{2,0,1:T(8,128)(2,1)S(1)} %multiply_convert_fusion) | data formatting | bytes 8388608 | tf_op jit(solution)/shard_map/convert_element_type | solution.py:34
  35.2 0.0 copy-start.1
  35.2 43.0 %all-to-all-start = ((bf16[8,32,64,128]{3,2,1,0:T(8,128)(2,1)}), bf16[8,32,64,128]{3,2,1,0:T(8,128)(2,1)}, u32[]{:S(2)}, u32[]{:S(2)}) async-start(bf16[8,32,64,128]{3,2,1,0:T(8,128)(2,1)} %bitcast.38), calls=%async_computation | async-start | bytes 8388608 | tf_op jit(solution)/shard_map/all_to_all | solution.py:35
  78.2 0.0 reduce-scatter.3.cloned.1.call-start
  78.2 0.0 copy-done.1
  78.2 48.9 %all-to-all-done = bf16[8,32,64,128]{3,2,1,0:T(8,128)(2,1)} async-done(((bf16[8,32,64,128]{3,2,1,0:T(8,128)(2,1)}), bf16[8,32,64,128]{3,2,1,0:T(8,128)(2,1)}, u32[]{:S(2)}, u32[]{:S(2)}) %all-to-all-start) | async-done | bytes 4194336 | tf_op jit(solution)/shard_map/all_to_all | solution.py:35
  127.1 10.0 %bitcast_multiply_fusion = f32[8,128,8,128]{3,1,2,0:T(8,128)} fusion(bf16[8,32,64,128]{3,2,1,0:T(8,128)(2,1)} %all-to-all-done), kind=kOutput, calls=%fused_computation.10 | convolution fusion | flops 4296015872 | bytes 8388608 | tf_op jit(solution)/shard_map/dot_general | solution.py:43
  137.1 4.9 %gather_fusion = f32[64,128,128]{2,1,0:T(8,128)} fusion(f32[64,128,128]{2,1,0:T(8,128)} %bitcast.39, s32[1024]{0:T(1024)S(1)} %pad_clamp_fusion), kind=kCustom, calls=%fused_computation | custom fusion | bytes 8388864 | tf_op jit(solution)/shard_map/jit(_take)/gather | solution.py:48
  142.0 4.5 %broadcast_select_fusion = f32[64,128,128]{2,1,0:T(8,128)} fusion(f32[64,128,128]{2,1,0:T(8,128)} %gather_fusion, pred[64]{0:T(512)(128)(4,1)S(1)} %compare_and_fusion), kind=kLoop, calls=%fused_computation.12 | loop fusion | flops 1048576 | bytes 8388672 | tf_op jit(solution)/shard_map/jit(_take)/select_n | solution.py:48
  146.5 0.0 reduce-scatter.3.cloned.1.call-update
  146.5 0.0 reduce-scatter.5.cloned.1.call-start
  146.6 215.5 %reduce-scatter.3.cloned.1.call-done = f32[2,128,128]{2,1,0:T(8,128)} async-done(((f32[64,128,128]{2,1,0:T(8,128)}), f32[2,128,128]{2,1,0:T(8,128)}) %reduce-scatter.3.cloned.1.call-update) | async-done | bytes 131088 | tf_op jit(solution)/shard_map/reduce_scatter | solution.py:49
  362.0 0.0 reduce-scatter.5.cloned.1.call-update
  362.1 36.6 %reduce-scatter.5.cloned.1.call-done = f32[2,16,128]{2,1,0:T(8,128)} async-done(((f32[2,128,128]{2,1,0:T(8,128)}), f32[2,16,128]{2,1,0:T(8,128)}) %reduce-scatter.5.cloned.1.call-update) | async-done | bytes 16400 | tf_op jit(solution)/shard_map/reduce_scatter | solution.py:50
  (3 shorter events, 0.0 us)
Async XLA Ops:
  8.5 4.3 %copy-start = (s32[1,4]{1,0:T(1,128)S(1)}, s32[1,4]{1,0:T(1,128)}, u32[]{:S(2)}) copy-start(s32[1,4]{1,0:T(1,128)} %param.11) | copy-start | bytes 52
  35.2 43.0 %copy-start.1 = (s32[64]{0:T(128)S(1)}, s32[64]{0:T(128)}, u32[]{:S(2)}) copy-start(s32[64]{0:T(128)} %param.13) | copy-start | bytes 772
  35.2 91.9 %all-to-all-start = ((bf16[8,32,64,128]{3,2,1,0:T(8,128)(2,1)}), bf16[8,32,64,128]{3,2,1,0:T(8,128)(2,1)}, u32[]{:S(2)}, u32[]{:S(2)}) async-start(bf16[8,32,64,128]{3,2,1,0:T(8,128)(2,1)} %bitcast.38), calls=%async_computation | async-start | bytes 8388608 | tf_op jit(solution)/shard_map/all_to_all | solution.py:35
  78.2 283.9 %reduce-scatter.3.cloned.1.call-start = ((), (), s32[]{:S(2)}) async-start(), calls=%async_computation.3 | async-start | bytes 4325376 | tf_op jit(solution)/shard_map/reduce_scatter | solution.py:49
  146.5 252.1 %reduce-scatter.5.cloned.1.call-start = ((), (), s32[]{:S(2)}) async-start(), calls=%async_computation.4 | async-start | bytes 147456 | tf_op jit(solution)/shard_map/reduce_scatter | solution.py:50
Sparse Core Ops, SparseCore 0:
  146.6 215.3 reduce-scatter.2
  364.7 33.9 reduce-scatter.4
where the time goes:
time: 407 us; the launch traced here: 405 us
  waiting for transfers between devices  301 us (74%)
  starting transfers between devices  43 us (11%)
  matrix products  18.5 us (5%)
  local copies, waits for them, and re-layouts  14.8 us (4%)
  between operations  13.5 us (3%)
  other arithmetic  11.5 us (3%)
    reduce_scatter x1, waiting for transfers between devices, shards(): shares = lax.psum_scatter(ordered, 'aux', scatter_dimension=0, tiled=True)  215 us
    all_to_all x1, waiting for transfers between devices, shards(): lax.all_to_all(halfway.reshape(occ_groups, orb_block, aux_rows, block_siz...  48.9 us
    all_to_all x1, starting transfers between devices, shards(): lax.all_to_all(halfway.reshape(occ_groups, orb_block, aux_rows, block_siz...  43 us
    reduce_scatter x1, waiting for transfers between devices, shards(): result = lax.psum_scatter(shares, 'occ', scatter_dimension=1, tiled=True)  36.6 us
    dot_general x1, matrix products, shards(): lax.dot_general(flat, flat, (((1,), (1,)), ((), ())), preferred_element_t...  10 us
    dot_general x1, matrix products, add_slot(): lax.dot_general(column, integrals, (((0,), (2,)), ((), ())), preferred_el...  8.54 us
  transfers between devices with their start and end apart: 3, of which 3 were waited for; matrix products, arithmetic and copies ran while one was open for 0% of the time, Pallas kernels for 0%

commit v1 on v0

v1 whole, which is shorter than its diff:
```python
import math

import jax
import jax.numpy as jnp
from jax import lax
from jax.experimental import pallas as pl
from jax.experimental.pallas import tpu as pltpu
from jax.sharding import PartitionSpec as P

MESH = pl.DeviceIdType.MESH
NX, NC, NY, NZ = 4, 2, 4, 8
NOCC = NX * NC
BLOCK = 128
SLOTS = 4
ORB = 256
AUX = 64
CHUNK = 16
PHASES = BLOCK // CHUNK
QD = AUX // NOCC
DEPTH = QD * ORB


def kernel(
    three_ref, coeff_ref, mask_ref, list_ref, count_ref, order_ref, out_ref,
    tbuf, cbuf, cm, sbuf, xbuf, hbuf, pack, crecv, yrecv, zrecv, b1, b2, fsend, frecv,
    tsem, csem, xss, xrs, css, crs, yss, yrs, zss, zrs, fss, frs,
):
    occ, aux = lax.axis_index("occ"), lax.axis_index("aux")
    x, c = occ // NC, occ % NC
    y, z = aux // NZ, aux % NZ

    def occ_to(e):
        return ((x + e // 2 + 1) % NX) * NC + (c + e) % NC

    def occ_from(e):
        return ((x + 2 * NX - e // 2 - 1) % NX) * NC + (c + e) % NC

    def at_occ(o):
        return (aux, o)

    def at_y(i):
        return (((y + i + 1) % NY) * NZ + z, occ)

    def at_z(i):
        return (y * NZ + (z + i + 1) % NZ, occ)

    barrier = pltpu.get_barrier_semaphore()
    for e in (0, 1, 2, 3, 4, 5, 7):
        pl.semaphore_signal(barrier, inc=1, device_id=at_occ(occ_to(e)), device_id_type=MESH)
    for i in range(NY - 1):
        pl.semaphore_signal(barrier, inc=1, device_id=at_y(i), device_id_type=MESH)
    for i in range(NZ - 1):
        pl.semaphore_signal(barrier, inc=1, device_id=at_z(i), device_id_type=MESH)

    def rows(t):
        return pl.ds(pl.multiple_of(t * CHUNK, CHUNK), CHUNK)

    def load(t):
        return pltpu.make_async_copy(three_ref.at[:, :, rows(t), :], tbuf.at[t], tsem.at[t])

    def x_copy(e, t):
        return pltpu.make_async_remote_copy(
            src_ref=sbuf.at[e, rows(t)], dst_ref=xbuf.at[occ, rows(t)],
            send_sem=xss.at[e, t], recv_sem=xrs.at[e, t],
            device_id=at_occ(occ_to(e)), device_id_type=MESH,
        )

    def x_arrival(e, t):
        return pltpu.make_async_remote_copy(
            src_ref=sbuf.at[e, rows(t)], dst_ref=xbuf.at[occ_from(e), rows(t)],
            send_sem=xss.at[e, t], recv_sem=xrs.at[e, t],
            device_id=at_occ(occ_to(e)), device_id_type=MESH,
        )

    def c_copy(t):
        return pltpu.make_async_remote_copy(
            src_ref=pack.at[t, 1 - c], dst_ref=crecv.at[t],
            send_sem=css.at[t], recv_sem=crs.at[t],
            device_id=at_occ(occ_to(7)), device_id_type=MESH,
        )

    def y_copy(t, i):
        return pltpu.make_async_remote_copy(
            src_ref=pack.at[t, c, (y + i + 1) % NY], dst_ref=yrecv.at[t, i],
            send_sem=yss.at[t, i], recv_sem=yrs.at[t, i],
            device_id=at_y(i), device_id_type=MESH,
        )

    def z_copy(t, i):
        return pltpu.make_async_remote_copy(
            src_ref=pack.at[t, c, y, (z + i + 1) % NZ], dst_ref=zrecv.at[t, i],
            send_sem=zss.at[t, i], recv_sem=zrs.at[t, i],
            device_id=at_z(i), device_id_type=MESH,
        )

    def loop(n, body):
        def step(i, carry):
            body(i)
            return carry

        lax.fori_loop(0, n, step, 0)

    coeff_copy = pltpu.make_async_copy(coeff_ref, cbuf, csem)
    coeff_copy.start()
    loop(PHASES, lambda t: load(t).start())

    group = lax.broadcasted_iota(jnp.int32, (1, ORB), 1) // (ORB // NOCC)
    hbuf[...] = jnp.zeros_like(hbuf)
    coeff_copy.wait()
    for s in range(SLOTS):
        n = list_ref[0, s]
        live = (s < count_ref[0, 0]).astype(jnp.int32)
        column = jnp.zeros((1, ORB), jnp.int32)
        for o in range(NOCC):
            column = jnp.where(group == o, mask_ref[n, o] * mask_ref[occ, o] * live, column)
        cm[pl.ds(s * BLOCK, BLOCK), :] = (cbuf[n].astype(jnp.float32) * column.astype(jnp.float32)).astype(jnp.bfloat16)

    def half(t, dest, target):
        first = pl.multiple_of(dest * QD, QD)
        left = jnp.concatenate(
            [tbuf[t, s, pl.ds(first, QD)].reshape(QD * CHUNK, BLOCK) for s in range(SLOTS)], axis=1
        )
        value = jnp.dot(left, cm[...], preferred_element_type=jnp.float32).astype(jnp.bfloat16)
        for q in range(QD):
            target[rows(t), pl.ds(q * ORB, ORB)] = value[q * CHUNK : (q + 1) * CHUNK]

    def send(e, t):
        half(t, occ_to(e), sbuf.at[e])
        x_copy(e, t).start()

    load(0).wait()
    half(0, occ_to(0), sbuf.at[0])
    half(0, occ_to(1), sbuf.at[1])
    pl.semaphore_wait(barrier, 7 + NY - 1 + NZ - 1)
    x_copy(0, 0).start()
    x_copy(1, 0).start()
    lax.fori_loop(2, 6, lambda e, v: (send(e, 0), v)[1], 0)
    send(7, 0)
    half(0, occ, xbuf.at[occ])

    def produce(t, carry):
        load(t).wait()
        loop(6, lambda e: send(e, t))
        send(7, t)
        half(t, occ, xbuf.at[occ])
        return carry

    lax.fori_loop(1, PHASES, produce, 0)

    def pair_sums(t):
        width = (t + 1) * CHUNK
        for e in (0, 1, 2, 3, 4, 5, 7):
            x_arrival(e, t).wait_recv()

        def one(n):
            left = xbuf[:, t * CHUNK : (t + 1) * CHUNK, :].reshape(NOCC * CHUNK, DEPTH)
            value = lax.dot_general(
                left, xbuf[n, :width, :], (((1,), (1,)), ((), ())), preferred_element_type=jnp.float32
            )
            hbuf[:, n, :, :width] = value.reshape(NOCC, CHUNK, width)

        loop(NOCC, one)

        def place(a):
            for parity in range(NC):
                o = order_ref[NC * a + parity]
                m, n = o // NOCC, o % NOCC
                pack[t, parity, a // NZ, a % NZ, :CHUNK, :] = hbuf[m, n]
                pack[t, parity, a // NZ, a % NZ, CHUNK:, :] = hbuf[n, m]

        loop(NY * NZ, place)
        c_copy(t).start()

    def after_core(t):
        c_copy(t).wait_recv()

        def one(i):
            pack[t, c, i] = pack[t, c, i] + crecv[t, i]

        loop(NY, one)
        loop(NY - 1, lambda i: y_copy(t, i).start())

    def after_y(t):
        loop(NY - 1, lambda i: y_copy(t, i).wait_recv())
        total = pack[t, c, y]
        for i in range(NY - 1):
            total = total + yrecv[t, i]
        pack[t, c, y] = total
        loop(NZ - 1, lambda i: z_copy(t, i).start())

    def after_z(t):
        loop(NZ - 1, lambda i: z_copy(t, i).wait_recv())
        total = pack[t, c, y, z]
        for i in range(NZ - 1):
            total = total + zrecv[t, i]
        b1[t * CHUNK : (t + 1) * CHUNK, :] = total[:CHUNK]
        b2[t * CHUNK : (t + 1) * CHUNK, :] = total[CHUNK:]

    for t in range(PHASES + 2):
        if t < PHASES:
            pair_sums(t)
        if t >= 2:
            after_z(t - 2)
        if 1 <= t <= PHASES:
            after_y(t - 1)
        if t < PHASES:
            after_core(t)

    p = lax.broadcasted_iota(jnp.int32, (BLOCK, BLOCK), 0)
    q = lax.broadcasted_iota(jnp.int32, (BLOCK, BLOCK), 1)
    whole = jnp.where(q < (p // CHUNK + 1) * CHUNK, b1[...], b2[...].T)
    fsend[...] = whole.reshape(NOCC, CHUNK, BLOCK)

    def f_copy(e):
        return pltpu.make_async_remote_copy(
            src_ref=fsend.at[occ_to(e)], dst_ref=frecv.at[occ],
            send_sem=fss.at[e], recv_sem=frs.at[e],
            device_id=at_occ(occ_to(e)), device_id_type=MESH,
        )

    for e in (0, 1, 2, 3, 4, 5, 7):
        f_copy(e).start()
    frecv[occ] = fsend[occ]

    def drain(t):
        loop(6, lambda e: x_copy(e, t).wait_send())
        x_copy(7, t).wait_send()
        c_copy(t).wait_send()
        loop(NY - 1, lambda i: y_copy(t, i).wait_send())
        loop(NZ - 1, lambda i: z_copy(t, i).wait_send())

    loop(PHASES, drain)
    for e in (0, 1, 2, 3, 4, 5, 7):
        f_copy(e).wait()
    scale = 1.0 / math.sqrt(AUX * NY * NZ * ORB)
    for parity in range(NC):
        total = frecv[parity]
        for i in range(1, NX):
            total = total + frecv[NC * i + parity]
        out_ref[parity] = total * scale


def shards(three_index, occ_coeff, occ_mask, screen_list, screen_count, owner_order):
    f32, bf16, dma = jnp.float32, jnp.bfloat16, pltpu.SemaphoreType.DMA
    smem = pl.BlockSpec(memory_space=pltpu.SMEM)
    anywhere = pl.BlockSpec(memory_space=pl.ANY)
    return pl.pallas_call(
        kernel,
        out_shape=jax.ShapeDtypeStruct((NC, CHUNK, BLOCK), f32),
        in_specs=[anywhere, anywhere, smem, smem, smem, smem],
        out_specs=pl.BlockSpec(memory_space=pltpu.VMEM),
        scratch_shapes=[
            pltpu.VMEM((PHASES, SLOTS, AUX, CHUNK, BLOCK), bf16),
            pltpu.VMEM((NOCC, BLOCK, ORB), bf16),
            pltpu.VMEM((SLOTS * BLOCK, ORB), bf16),
            pltpu.VMEM((NOCC, BLOCK, DEPTH), bf16),
            pltpu.VMEM((NOCC, BLOCK, DEPTH), bf16),
            pltpu.VMEM((NOCC, NOCC, CHUNK, BLOCK), f32),
            pltpu.VMEM((PHASES, NC, NY, NZ, 2 * CHUNK, BLOCK), f32),
            pltpu.VMEM((PHASES, NY, NZ, 2 * CHUNK, BLOCK), f32),
            pltpu.VMEM((PHASES, NY - 1, NZ, 2 * CHUNK, BLOCK), f32),
            pltpu.VMEM((PHASES, NZ - 1, 2 * CHUNK, BLOCK), f32),
            pltpu.VMEM((BLOCK, BLOCK), f32),
            pltpu.VMEM((BLOCK, BLOCK), f32),
            pltpu.VMEM((NOCC, CHUNK, BLOCK), f32),
            pltpu.VMEM((NOCC, CHUNK, BLOCK), f32),
            dma((PHASES,)),
            dma,
            dma((8, PHASES)),
            dma((8, PHASES)),
            dma((PHASES,)),
            dma((PHASES,)),
            dma((PHASES, NY - 1)),
            dma((PHASES, NY - 1)),
            dma((PHASES, NZ - 1)),
            dma((PHASES, NZ - 1)),
            dma((8,)),
            dma((8,)),
        ],
        compiler_params=pltpu.CompilerParams(
            collective_id=0, has_side_effects=True, vmem_limit_bytes=56 * 1024 * 1024
        ),
        name="exchange",
    )(three_index, occ_coeff.reshape(NOCC, BLOCK, ORB), occ_mask, screen_list, screen_count, owner_order)


def solution(mesh):
    in_specs = (P("occ", "aux", None, None), P(), P(), P("aux", "occ"), P("aux", "occ"), P())
    out_specs = P("aux", "occ", None)
    return jax.shard_map(shards, mesh=mesh, in_specs=in_specs, out_specs=out_specs, check_vma=False)
```

time: 407 us -> 107 us (0.26)
  waiting for transfers between devices: 301 us -> 0 us
  Pallas kernels: 0 us -> 105 us
  starting transfers between devices: 43 us -> 0 us
  matrix products: 18.5 us -> 0 us
  local copies, waits for them, and re-layouts: 14.8 us -> 1.32 us
  between operations: 13.5 us -> 0.66 us
  other arithmetic: 11.5 us -> 0 us
    reduce_scatter x2 -> x0, waiting for transfers between devices: 252 us -> none  [the longest x1 215 us: shards(): shares = lax.psum_scatter(ordered, 'aux', scatter_dimension=0, tiled=True)]
    pallas_call x0 -> x1, Pallas kernels: none -> 105 us  [shards(): pl.pallas_call(kernel, out_shape=jax.ShapeDtypeStruct((NC, CHUNK, BLOCK),...]
    all_to_all x1 -> x0, waiting for transfers between devices: 48.9 us -> none  [shards(): lax.all_to_all(halfway.reshape(occ_groups, orb_block, aux_rows, block_siz...]
    all_to_all x1 -> x0, starting transfers between devices: 43 us -> none  [shards(): lax.all_to_all(halfway.reshape(occ_groups, orb_block, aux_rows, block_siz...]
    dot_general x2 -> x0, matrix products: 18.5 us -> none  [the longest x1 10 us: shards(): lax.dot_general(flat, flat, (((1,), (1,)), ((), ())), preferred_element_t...]
    convert_element_type x3 -> x0, other arithmetic: 5.93 us -> none  [the longest x1 4.54 us: shards(): halfway = (accum * row_mask[:, None, None]).astype(jnp.bfloat16)]
    gather x1 -> x0, local copies, waits for them, and re-layouts: 4.93 us -> none  [shards(): ordered = jnp.take(blocks, owner_order, axis=0)]
    convert_element_type x3 -> x0, local copies, waits for them, and re-layouts: 4.85 us -> none  [the longest x1 4.68 us: shards(): halfway = (accum * row_mask[:, None, None]).astype(jnp.bfloat16)]
  transfers between devices with their start and end apart: 3 -> 0, of which waited for: 3 -> 0; matrix products, arithmetic and copies ran while one was open for 0% -> 0% of each run, Pallas kernels for 0% -> 0%
where the time goes in v1:
time: 107 us
  Pallas kernels  105 us (98%)
  local copies, waits for them, and re-layouts  1.32 us (1%)
    pallas_call x1, Pallas kernels, shards(): pl.pallas_call(kernel, out_shape=jax.ShapeDtypeStruct((NC, CHUNK, BLOCK),...  105 us

profile of v1, /device:TPU:1, one launch (start us, length us, event | category | flops | bytes accessed | tf_op | source)
XLA Modules:
  0.0 106.6 jit_solution(3175393321705623148)
XLA Ops:
  0.7 104.6 %exchange.1 = f32[2,16,128]{2,1,0:T(8,128)} custom-call(bf16[4,64,128,128]{3,2,1,0:T(8,128)(2,1)} %three_ref.1, bf16[8,128,256]{2,1,0:T(8,128)(2,1)} %bitcast.1, s32[8,8]{1,0:T(8,128)} %mask_ref.1, s32[1,4]{1,0:T(1,128)} %list_ref.1, s32[1,1]{1,0:T(1,128)S(6)} %copy.8.count_ref, s32[64]{0:T(128)} %order_ref.1), custom_call_target="tpu_custom_call" | custom-call | tf_op jit(solution)/shard_map/exchange/pallas_call | solution.py:247
  105.2 1.3 %copy.9 = f32[2,16,128]{2,1,0:T(8,128)} copy(f32[2,16,128]{2,1,0:T(8,128)} %exchange.1) | data formatting | bytes 32768

commit v2 on v1

--- a/solution.py
+++ b/solution.py
@@ -18,11 +18,15 @@
 PHASES = BLOCK // CHUNK
 QD = AUX // NOCC
 DEPTH = QD * ORB
+STEPS = ((2, 0), (2, 1), (1, 0), (3, 0), (1, 1), (3, 1), (0, 1))
+PARTNERS = range(len(STEPS))
+MATE = len(STEPS) - 1
+HALF = PHASES // 2
 
 
 def kernel(
     three_ref, coeff_ref, mask_ref, list_ref, count_ref, order_ref, out_ref,
-    tbuf, cbuf, cm, sbuf, xbuf, hbuf, pack, crecv, yrecv, zrecv, b1, b2, fsend, frecv,
+    tbuf, cbuf, cm, sbuf, xbuf, wbuf, rbuf, hbuf, early, early_c, early_y, early_z, late, late_c, late_y, late_z, b1, b2, fsend, frecv,
     tsem, csem, xss, xrs, css, crs, yss, yrs, zss, zrs, fss, frs,
 ):
     occ, aux = lax.axis_index("occ"), lax.axis_index("aux")
@@ -30,10 +34,10 @@
     y, z = aux // NZ, aux % NZ
 
     def occ_to(e):
-        return ((x + e // 2 + 1) % NX) * NC + (c + e) % NC
+        return ((x + STEPS[e][0]) % NX) * NC + (c + STEPS[e][1]) % NC
 
     def occ_from(e):
-        return ((x + 2 * NX - e // 2 - 1) % NX) * NC + (c + e) % NC
+        return ((x + NX - STEPS[e][0]) % NX) * NC + (c + STEPS[e][1]) % NC
 
     def at_occ(o):
         return (aux, o)
@@ -45,7 +49,7 @@
         return (y * NZ + (z + i + 1) % NZ, occ)
 
     barrier = pltpu.get_barrier_semaphore()
-    for e in (0, 1, 2, 3, 4, 5, 7):
+    for e in PARTNERS:
         pl.semaphore_signal(barrier, inc=1, device_id=at_occ(occ_to(e)), device_id_type=MESH)
     for i in range(NY - 1):
         pl.semaphore_signal(barrier, inc=1, device_id=at_y(i), device_id_type=MESH)
@@ -72,23 +76,31 @@
             device_id=at_occ(occ_to(e)), device_id_type=MESH,
         )
 
+    def packs(t):
+        if t < HALF:
+            return early.at[t], early_c.at[t], early_y.at[t], early_z.at[t]
+        return late.at[t - HALF], late_c.at[t - HALF], late_y.at[t - HALF], late_z.at[t - HALF]
+
     def c_copy(t):
-        return pltpu.make_async_remote_copy(
-            src_ref=pack.at[t, 1 - c], dst_ref=crecv.at[t],
+        pack, crecv, _, _ = packs(t)
+        return pltpu.make_async_remote_copy(
+            src_ref=pack.at[1 - c], dst_ref=crecv,
             send_sem=css.at[t], recv_sem=crs.at[t],
-            device_id=at_occ(occ_to(7)), device_id_type=MESH,
+            device_id=at_occ(occ_to(MATE)), device_id_type=MESH,
         )
 
     def y_copy(t, i):
-        return pltpu.make_async_remote_copy(
-            src_ref=pack.at[t, c, (y + i + 1) % NY], dst_ref=yrecv.at[t, i],
+        pack, _, yrecv, _ = packs(t)
+        return pltpu.make_async_remote_copy(
+            src_ref=pack.at[c, (y + i + 1) % NY], dst_ref=yrecv.at[i],
             send_sem=yss.at[t, i], recv_sem=yrs.at[t, i],
             device_id=at_y(i), device_id_type=MESH,
         )
 
     def z_copy(t, i):
-        return pltpu.make_async_remote_copy(
-            src_ref=pack.at[t, c, y, (z + i + 1) % NZ], dst_ref=zrecv.at[t, i],
+        pack, _, _, zrecv = packs(t)
+        return pltpu.make_async_remote_copy(
+            src_ref=pack.at[c, y, (z + i + 1) % NZ], dst_ref=zrecv.at[i],
             send_sem=zss.at[t, i], recv_sem=zrs.at[t, i],
             device_id=at_z(i), device_id_type=MESH,
         )
@@ -105,7 +117,6 @@
     loop(PHASES, lambda t: load(t).start())
 
     group = lax.broadcasted_iota(jnp.int32, (1, ORB), 1) // (ORB // NOCC)
-    hbuf[...] = jnp.zeros_like(hbuf)
     coeff_copy.wait()
     for s in range(SLOTS):
         n = list_ref[0, s]
@@ -129,82 +140,110 @@
         x_copy(e, t).start()
 
     load(0).wait()
-    half(0, occ_to(0), sbuf.at[0])
-    half(0, occ_to(1), sbuf.at[1])
-    pl.semaphore_wait(barrier, 7 + NY - 1 + NZ - 1)
-    x_copy(0, 0).start()
-    x_copy(1, 0).start()
-    lax.fori_loop(2, 6, lambda e, v: (send(e, 0), v)[1], 0)
-    send(7, 0)
+    for e in range(4):
+        half(0, occ_to(e), sbuf.at[e])
+    pl.semaphore_wait(barrier, len(STEPS) + NY - 1 + NZ - 1)
+    for e in range(4):
+        x_copy(e, 0).start()
+    for e in PARTNERS[4:]:
+        send(e, 0)
     half(0, occ, xbuf.at[occ])
 
     def produce(t, carry):
         load(t).wait()
-        loop(6, lambda e: send(e, t))
-        send(7, t)
+        for e in PARTNERS:
+            send(e, t)
         half(t, occ, xbuf.at[occ])
         return carry
 
     lax.fori_loop(1, PHASES, produce, 0)
 
     def pair_sums(t):
-        width = (t + 1) * CHUNK
-        for e in (0, 1, 2, 3, 4, 5, 7):
+        for e in PARTNERS:
             x_arrival(e, t).wait_recv()
-
-        def one(n):
-            left = xbuf[:, t * CHUNK : (t + 1) * CHUNK, :].reshape(NOCC * CHUNK, DEPTH)
-            value = lax.dot_general(
-                left, xbuf[n, :width, :], (((1,), (1,)), ((), ())), preferred_element_type=jnp.float32
-            )
-            hbuf[:, n, :, :width] = value.reshape(NOCC, CHUNK, width)
-
-        loop(NOCC, one)
-
-        def place(a):
-            for parity in range(NC):
+        left = xbuf[:, t * CHUNK : (t + 1) * CHUNK, :].reshape(BLOCK, DEPTH)
+
+        for i in range(QD):
+            wbuf[t // 2, i * ORB : (i + 1) * ORB, t % 2 * BLOCK : (t % 2 + 1) * BLOCK] = left[:, i * ORB : (i + 1) * ORB].T
+
+        def product(u):
+            value = jnp.dot(left, wbuf[u], preferred_element_type=jnp.float32)
+            rbuf[2 * u] = value[:, :BLOCK].reshape(NOCC, CHUNK, BLOCK)
+            rbuf[2 * u + 1] = value[:, BLOCK:].reshape(NOCC, CHUNK, BLOCK)
+
+        loop(t // 2 + 1, product)
+
+        if t >= 2:
+            after_y(t - 2)
+
+        segment = lax.broadcasted_iota(jnp.int32, (CHUNK, BLOCK), 1) // CHUNK
+
+        for d in (1, 2, 4):
+            low = segment & d == 0
+            for m in range(NOCC):
+                for i in range(PHASES):
+                    if i & d == 0:
+                        one, two = rbuf[i, m], rbuf[i + d, m]
+                        first = jnp.where(low, one, pltpu.roll(two, d * CHUNK, 1))
+                        second = jnp.where(low, pltpu.roll(one, BLOCK - d * CHUNK, 1), two)
+                        if d < 4:
+                            rbuf[i, m], rbuf[i + d, m] = first, second
+                        else:
+                            hbuf[m, i], hbuf[m, i + d] = first, second
+
+        def place(g):
+            for k in range(NC * NZ // 2):
+                a, parity = g * (NZ // 2) + k // NC, k % NC
                 o = order_ref[NC * a + parity]
-                m, n = o // NOCC, o % NOCC
-                pack[t, parity, a // NZ, a % NZ, :CHUNK, :] = hbuf[m, n]
-                pack[t, parity, a // NZ, a % NZ, CHUNK:, :] = hbuf[n, m]
-
-        loop(NY * NZ, place)
+                m, n = o >> 3, o & 7
+                if t < HALF:
+                    turned = pltpu.roll(hbuf[n, m], BLOCK // 2, 1)
+                    early[t, parity, a // NZ, a % NZ] = jnp.where(segment < HALF, hbuf[m, n], turned)
+                else:
+                    late[t - HALF, parity, a // NZ, a % NZ, :CHUNK] = hbuf[m, n]
+                    late[t - HALF, parity, a // NZ, a % NZ, CHUNK:] = hbuf[n, m]
+
+        loop(2 * NY, place)
         c_copy(t).start()
 
     def after_core(t):
+        pack, crecv, _, _ = packs(t)
         c_copy(t).wait_recv()
 
         def one(i):
-            pack[t, c, i] = pack[t, c, i] + crecv[t, i]
+            pack[c, i] = pack[c, i] + crecv[i]
 
         loop(NY, one)
         loop(NY - 1, lambda i: y_copy(t, i).start())
 
     def after_y(t):
+        pack, _, yrecv, _ = packs(t)
         loop(NY - 1, lambda i: y_copy(t, i).wait_recv())
-        total = pack[t, c, y]
+        total = pack[c, y]
         for i in range(NY - 1):
-            total = total + yrecv[t, i]
-        pack[t, c, y] = total
+            total = total + yrecv[i]
+        pack[c, y] = total
         loop(NZ - 1, lambda i: z_copy(t, i).start())
 
     def after_z(t):
+        pack, _, _, zrecv = packs(t)
         loop(NZ - 1, lambda i: z_copy(t, i).wait_recv())
-        total = pack[t, c, y, z]
+        total = pack[c, y, z]
         for i in range(NZ - 1):
-            total = total + zrecv[t, i]
+            total = total + zrecv[i]
         b1[t * CHUNK : (t + 1) * CHUNK, :] = total[:CHUNK]
-        b2[t * CHUNK : (t + 1) * CHUNK, :] = total[CHUNK:]
-
-    for t in range(PHASES + 2):
-        if t < PHASES:
-            pair_sums(t)
-        if t >= 2:
-            after_z(t - 2)
-        if 1 <= t <= PHASES:
-            after_y(t - 1)
-        if t < PHASES:
-            after_core(t)
+        b2[t * CHUNK : (t + 1) * CHUNK, :] = pltpu.roll(total, BLOCK // 2, 1) if t < HALF else total[CHUNK:]
+
+    for t in range(PHASES):
+        pair_sums(t)
+        if t >= 3:
+            after_z(t - 3)
+        after_core(t)
+    after_y(PHASES - 2)
+    after_z(PHASES - 3)
+    after_y(PHASES - 1)
+    after_z(PHASES - 2)
+    after_z(PHASES - 1)
 
     p = lax.broadcasted_iota(jnp.int32, (BLOCK, BLOCK), 0)
     q = lax.broadcasted_iota(jnp.int32, (BLOCK, BLOCK), 1)
@@ -218,19 +257,17 @@
             device_id=at_occ(occ_to(e)), device_id_type=MESH,
         )
 
-    for e in (0, 1, 2, 3, 4, 5, 7):
+    for e in PARTNERS:
         f_copy(e).start()
     frecv[occ] = fsend[occ]
 
-    def drain(t):
-        loop(6, lambda e: x_copy(e, t).wait_send())
-        x_copy(7, t).wait_send()
+    for t in range(PHASES):
+        for e in PARTNERS:
+            x_copy(e, t).wait_send()
         c_copy(t).wait_send()
         loop(NY - 1, lambda i: y_copy(t, i).wait_send())
         loop(NZ - 1, lambda i: z_copy(t, i).wait_send())
-
-    loop(PHASES, drain)
-    for e in (0, 1, 2, 3, 4, 5, 7):
+    for e in PARTNERS:
         f_copy(e).wait()
     scale = 1.0 / math.sqrt(AUX * NY * NZ * ORB)
     for parity in range(NC):
@@ -253,29 +290,32 @@
             pltpu.VMEM((PHASES, SLOTS, AUX, CHUNK, BLOCK), bf16),
             pltpu.VMEM((NOCC, BLOCK, ORB), bf16),
             pltpu.VMEM((SLOTS * BLOCK, ORB), bf16),
+            pltpu.VMEM((len(STEPS), BLOCK, DEPTH), bf16),
             pltpu.VMEM((NOCC, BLOCK, DEPTH), bf16),
-            pltpu.VMEM((NOCC, BLOCK, DEPTH), bf16),
+            pltpu.VMEM((PHASES // 2, DEPTH, 2 * BLOCK), bf16),
+            pltpu.VMEM((PHASES, NOCC, CHUNK, BLOCK), f32),
             pltpu.VMEM((NOCC, NOCC, CHUNK, BLOCK), f32),
-            pltpu.VMEM((PHASES, NC, NY, NZ, 2 * CHUNK, BLOCK), f32),
-            pltpu.VMEM((PHASES, NY, NZ, 2 * CHUNK, BLOCK), f32),
-            pltpu.VMEM((PHASES, NY - 1, NZ, 2 * CHUNK, BLOCK), f32),
-            pltpu.VMEM((PHASES, NZ - 1, 2 * CHUNK, BLOCK), f32),
+            *(
+                pltpu.VMEM((HALF, *lead, height, BLOCK), f32)
+                for height in (CHUNK, 2 * CHUNK)
+                for lead in ((NC, NY, NZ), (NY, NZ), (NY - 1, NZ), (NZ - 1,))
+            ),
             pltpu.VMEM((BLOCK, BLOCK), f32),
             pltpu.VMEM((BLOCK, BLOCK), f32),
             pltpu.VMEM((NOCC, CHUNK, BLOCK), f32),
             pltpu.VMEM((NOCC, CHUNK, BLOCK), f32),
             dma((PHASES,)),
             dma,
-            dma((8, PHASES)),
-            dma((8, PHASES)),
+            dma((len(STEPS), PHASES)),
+            dma((len(STEPS), PHASES)),
             dma((PHASES,)),
             dma((PHASES,)),
             dma((PHASES, NY - 1)),
             dma((PHASES, NY - 1)),
             dma((PHASES, NZ - 1)),
             dma((PHASES, NZ - 1)),
-            dma((8,)),
-            dma((8,)),
+            dma((len(STEPS),)),
+            dma((len(STEPS),)),
         ],
         compiler_params=pltpu.CompilerParams(
             collective_id=0, has_side_effects=True, vmem_limit_bytes=56 * 1024 * 1024

time: 107 us -> 85.5 us (0.80)
  Pallas kernels: 105 us -> 83.3 us
    pallas_call x1, Pallas kernels: 105 us -> 83.3 us  [shards(): pl.pallas_call(kernel, out_shape=jax.ShapeDtypeStruct((NC, CHUNK, BLOCK),...]
where the time goes in v2:
time: 85.5 us; the launch traced here: 85.3 us
  Pallas kernels  83.3 us (97%)
  local copies, waits for them, and re-layouts  1.32 us (2%)
    pallas_call x1, Pallas kernels, shards(): pl.pallas_call(kernel, out_shape=jax.ShapeDtypeStruct((NC, CHUNK, BLOCK),...  83.3 us

profile of v2, /device:TPU:1, one launch (start us, length us, event | category | flops | bytes accessed | tf_op | source)
XLA Modules:
  0.0 85.3 jit_solution(5552117548383139470)
XLA Ops:
  0.7 83.3 %exchange.1 = f32[2,16,128]{2,1,0:T(8,128)} custom-call(bf16[4,64,128,128]{3,2,1,0:T(8,128)(2,1)} %three_ref.1, bf16[8,128,256]{2,1,0:T(8,128)(2,1)} %bitcast.1, s32[8,8]{1,0:T(8,128)} %mask_ref.1, s32[1,4]{1,0:T(1,128)} %list_ref.1, s32[1,1]{1,0:T(1,128)S(6)} %copy.8.count_ref, s32[64]{0:T(128)} %order_ref.1), custom_call_target="tpu_custom_call" | custom-call | tf_op jit(solution)/shard_map/exchange/pallas_call | solution.py:284
  84.0 1.3 %copy.9 = f32[2,16,128]{2,1,0:T(8,128)} copy(f32[2,16,128]{2,1,0:T(8,128)} %exchange.1) | data formatting | bytes 32768

commit v3 on v2

v3 whole, which is shorter than its diff:
```python
import math

import jax
import jax.numpy as jnp
from jax import lax
from jax.experimental import pallas as pl
from jax.experimental.pallas import tpu as pltpu
from jax.sharding import PartitionSpec as P

MESH = pl.DeviceIdType.MESH
NX, NC, NY, NZ = 4, 2, 4, 8
NOCC = NX * NC
BLOCK = 128
SLOTS = 4
ORB = 256
AUX = 64
CHUNK = 16
SUB = CHUNK // 2
CHUNKS = BLOCK // CHUNK
FULL = CHUNKS - 1
PHASES = FULL + 2
QD = AUX // NOCC
DEPTH = QD * ORB
START = (*range(0, BLOCK - CHUNK + 1, CHUNK), BLOCK - SUB, BLOCK)
Y_STEPS = (2, 1, 3)
Z_STEPS = (4, 3, 5, 2, 6, 1, 7)
STEPS = ((2, 0), (2, 1), (1, 0), (3, 0), (1, 1), (3, 1), (0, 1))
PARTNERS = range(len(STEPS))
MATE = len(STEPS) - 1
HALF = CHUNKS // 2


def kernel(
    three_ref, coeff_ref, mask_ref, list_ref, count_ref, order_ref, out_ref,
    tbuf, cbuf, cm, sbuf, xbuf, ssub, xsub, wbuf, wsub, rbuf, hbuf, early, early_c, early_y, early_z, late, late_c, late_y, late_z, last, last_c, last_y, last_z, b1, b2, fsend, frecv,
    tsem, fsem, csem, xss, xrs, css, crs, yss, yrs, zss, zrs, fss, frs,
):
    occ, aux = lax.axis_index("occ"), lax.axis_index("aux")
    x, c = occ // NC, occ % NC
    y, z = aux // NZ, aux % NZ

    def occ_to(e):
        return ((x + STEPS[e][0]) % NX) * NC + (c + STEPS[e][1]) % NC

    def occ_from(e):
        return ((x + NX - STEPS[e][0]) % NX) * NC + (c + STEPS[e][1]) % NC

    def at_occ(o):
        return (aux, o)

    def at_y(i):
        return (((y + Y_STEPS[i]) % NY) * NZ + z, occ)

    def at_z(i):
        return (y * NZ + (z + Z_STEPS[i]) % NZ, occ)

    barrier = pltpu.get_barrier_semaphore()
    for e in PARTNERS:
        pl.semaphore_signal(barrier, inc=1, device_id=at_occ(occ_to(e)), device_id_type=MESH)
    for i in range(NY - 1):
        pl.semaphore_signal(barrier, inc=1, device_id=at_y(i), device_id_type=MESH)
    for i in range(NZ - 1):
        pl.semaphore_signal(barrier, inc=1, device_id=at_z(i), device_id_type=MESH)

    def rows(t):
        return pl.ds(pl.multiple_of(t * CHUNK, CHUNK), CHUNK)

    def load(t):
        return pltpu.make_async_copy(three_ref.at[:, :, rows(t), :], tbuf.at[t], tsem.at[t])

    def load_first(d):
        at = pl.ds(pl.multiple_of(d * QD, QD), QD)
        return pltpu.make_async_copy(three_ref.at[:, at, :CHUNK, :], tbuf.at[0, :, at], fsem.at[d])

    def x_ends(e, t, sender):
        if isinstance(t, int) and t >= FULL:
            return ssub.at[e, t - FULL], xsub.at[t - FULL, sender]
        return sbuf.at[e, rows(t)], xbuf.at[sender, rows(t)]

    def x_copy(e, t):
        source, target = x_ends(e, t, occ)
        return pltpu.make_async_remote_copy(
            src_ref=source, dst_ref=target,
            send_sem=xss.at[e, t], recv_sem=xrs.at[e, t],
            device_id=at_occ(occ_to(e)), device_id_type=MESH,
        )

    def x_arrival(e, t):
        source, target = x_ends(e, t, occ_from(e))
        return pltpu.make_async_remote_copy(
            src_ref=source, dst_ref=target,
            send_sem=xss.at[e, t], recv_sem=xrs.at[e, t],
            device_id=at_occ(occ_to(e)), device_id_type=MESH,
        )

    def packs(t):
        if t < HALF:
            return early.at[t], early_c.at[t], early_y.at[t], early_z.at[t]
        if t < FULL:
            return late.at[t - HALF], late_c.at[t - HALF], late_y.at[t - HALF], late_z.at[t - HALF]
        return last.at[t - FULL], last_c.at[t - FULL], last_y.at[t - FULL], last_z.at[t - FULL]

    def group_of(i):
        return (y + Y_STEPS[i]) % NY if i < NY - 1 else y

    def c_copy(t, i):
        pack, crecv, _, _ = packs(t)
        at = group_of(i)
        return pltpu.make_async_remote_copy(
            src_ref=pack.at[1 - c, at], dst_ref=crecv.at[at],
            send_sem=css.at[t, i], recv_sem=crs.at[t, i],
            device_id=at_occ(occ_to(MATE)), device_id_type=MESH,
        )

    def y_copy(t, i):
        pack, _, yrecv, _ = packs(t)
        return pltpu.make_async_remote_copy(
            src_ref=pack.at[c, group_of(i)], dst_ref=yrecv.at[i],
            send_sem=yss.at[t, i], recv_sem=yrs.at[t, i],
            device_id=at_y(i), device_id_type=MESH,
        )

    def z_copy(t, i):
        pack, _, _, zrecv = packs(t)
        return pltpu.make_async_remote_copy(
            src_ref=pack.at[c, y, (z + Z_STEPS[i]) % NZ], dst_ref=zrecv.at[i],
            send_sem=zss.at[t, i], recv_sem=zrs.at[t, i],
            device_id=at_z(i), device_id_type=MESH,
        )

    def loop(n, body):
        def step(i, carry):
            body(i)
            return carry

        lax.fori_loop(0, n, step, 0)

    coeff_copy = pltpu.make_async_copy(coeff_ref, cbuf, csem)
    coeff_copy.start()
    for e in PARTNERS:
        load_first(occ_to(e)).start()
    load_first(occ).start()

    group = lax.broadcasted_iota(jnp.int32, (1, ORB), 1) // (ORB // NOCC)
    coeff_copy.wait()
    for s in range(SLOTS):
        n = list_ref[0, s]
        live = (s < count_ref[0, 0]).astype(jnp.int32)
        column = jnp.zeros((1, ORB), jnp.int32)
        for o in range(NOCC):
            column = jnp.where(group == o, mask_ref[n, o] * mask_ref[occ, o] * live, column)
        cm[pl.ds(s * BLOCK, BLOCK), :] = (cbuf[n].astype(jnp.float32) * column.astype(jnp.float32)).astype(jnp.bfloat16)

    def half_rows(t, dest):
        first = pl.multiple_of(dest * QD, QD)
        left = jnp.concatenate(
            [tbuf[t, s, pl.ds(first, QD)].reshape(QD * CHUNK, BLOCK) for s in range(SLOTS)], axis=1
        )
        return jnp.dot(left, cm[...], preferred_element_type=jnp.float32)

    def half(t, dest, target):
        value = half_rows(t, dest).astype(jnp.bfloat16)
        for q in range(QD):
            target[rows(t), pl.ds(q * ORB, ORB)] = value[q * CHUNK : (q + 1) * CHUNK]

    def half_last(dest, targets):
        value = half_rows(FULL, dest).reshape(QD, 2, SUB, ORB)
        for s, target in enumerate(targets):
            for q in range(QD // 2):
                pair = jnp.concatenate([value[q, s], value[q + QD // 2, s]], axis=0)
                target[:, q * ORB : (q + 1) * ORB] = pair.astype(jnp.bfloat16)

    def send(e, t):
        half(t, occ_to(e), sbuf.at[e])
        x_copy(e, t).start()

    for e in PARTNERS:
        load_first(occ_to(e)).wait()
        half(0, occ_to(e), sbuf.at[e])
        if e == 3:
            lax.fori_loop(1, CHUNKS, lambda t, v: (load(t).start(), v)[1], 0)
            pl.semaphore_wait(barrier, len(STEPS) + NY - 1 + NZ - 1)
            for i in range(e):
                x_copy(i, 0).start()
        if e >= 3:
            x_copy(e, 0).start()
    load_first(occ).wait()
    half(0, occ, xbuf.at[occ])

    def produce(t, carry):
        load(t).wait()
        for e in PARTNERS:
            send(e, t)
        half(t, occ, xbuf.at[occ])
        return carry

    lax.fori_loop(1, FULL, produce, 0)
    load(FULL).wait()
    for e in PARTNERS:
        half_last(occ_to(e), (ssub.at[e, 0], ssub.at[e, 1]))
        x_copy(e, FULL).start()
    for e in PARTNERS:
        x_copy(e, FULL + 1).start()
    half_last(occ, (xsub.at[0, occ], xsub.at[1, occ]))

    def pair_sums(t):
        for e in PARTNERS:
            x_arrival(e, t).wait_recv()
        height = START[t + 1] - START[t]
        if t < FULL:
            left = xbuf[:, t * CHUNK : (t + 1) * CHUNK, :].reshape(BLOCK, DEPTH)
            for i in range(QD):
                wbuf[t // 2, i * ORB : (i + 1) * ORB, t % 2 * BLOCK : (t % 2 + 1) * BLOCK] = left[:, i * ORB : (i + 1) * ORB].T
            for u in range(t // 2 + 1):
                value = jnp.dot(left, wbuf[u], preferred_element_type=jnp.float32)
                rbuf[2 * u] = value[:, :BLOCK].reshape(NOCC, CHUNK, BLOCK)
                rbuf[2 * u + 1] = value[:, BLOCK:].reshape(NOCC, CHUNK, BLOCK)
        else:
            left = xsub[t - FULL].reshape(BLOCK, DEPTH // 2)
            for i in range(QD // 2):
                wsub[t - FULL, i * ORB : (i + 1) * ORB, :] = left[:, i * ORB : (i + 1) * ORB].T

            def halves(value):
                value = value.reshape(NOCC, 2, SUB, value.shape[1])
                return value[:, 0], value[:, 1]

            for u in range(CHUNKS // 2):
                wide = slice(0, 2 * BLOCK if 2 * u + 1 < FULL else BLOCK)
                low = jnp.dot(left, wbuf[u, : DEPTH // 2, wide], preferred_element_type=jnp.float32)
                high = jnp.dot(left, wbuf[u, DEPTH // 2 :, wide], preferred_element_type=jnp.float32)
                value = halves(low)[0] + halves(high)[1]
                rbuf[2 * u, :, :SUB] = value[:, :, :BLOCK]
                if 2 * u + 1 < FULL:
                    rbuf[2 * u + 1, :, :SUB] = value[:, :, BLOCK:]
            low, high = halves(jnp.dot(left, wsub[0], preferred_element_type=jnp.float32))
            value = low + pltpu.roll(high, BLOCK - SUB, 2)
            if t > FULL:
                low, high = halves(jnp.dot(left, wsub[1], preferred_element_type=jnp.float32))
                lane = lax.broadcasted_iota(jnp.int32, (NOCC, SUB, BLOCK), 2)
                value = jnp.where(lane % CHUNK < SUB, value, pltpu.roll(low, SUB, 2) + high)
            rbuf[FULL, :, :SUB] = value

        if 2 <= t < PHASES - 1:
            after_y(t - 2)

        segment = lax.broadcasted_iota(jnp.int32, (height, BLOCK), 1) // CHUNK

        for d in (1, 2, 4):
            low = segment & d == 0
            for m in range(NOCC):
                for i in range(CHUNKS):
                    if i & d == 0:
                        one, two = rbuf[i, m, :height], rbuf[i + d, m, :height]
                        first = jnp.where(low, one, pltpu.roll(two, d * CHUNK, 1))
                        second = jnp.where(low, pltpu.roll(one, BLOCK - d * CHUNK, 1), two)
                        if d < 4:
                            rbuf[i, m, :height], rbuf[i + d, m, :height] = first, second
                        else:
                            hbuf[m, i, :height], hbuf[m, i + d, :height] = first, second

        pack = packs(t)[0]
        for i in range(NY):
            group = group_of(i)
            for k in range(NC * NZ):
                at, parity = k // NC, k % NC
                o = order_ref[NC * NZ * group + k]
                m, n = o >> 3, o & 7
                if t < HALF:
                    turned = pltpu.roll(hbuf[n, m], BLOCK // 2, 1)
                    pack[parity, group, at] = jnp.where(segment < HALF, hbuf[m, n], turned)
                else:
                    pack[parity, group, at, :height] = hbuf[m, n, :height]
                    pack[parity, group, at, height:] = hbuf[n, m, :height]
            c_copy(t, i).start()

    def after_core(t):
        pack, crecv, _, _ = packs(t)
        for i in range(NY):
            at = group_of(i)
            c_copy(t, i).wait_recv()
            pack[c, at] = pack[c, at] + crecv[at]
            if i < NY - 1:
                y_copy(t, i).start()

    def after_y(t):
        pack, _, yrecv, _ = packs(t)
        for i in range(NY - 1):
            y_copy(t, i).wait_recv()
        total = pack[c, y]
        for i in range(NY - 1):
            total = total + yrecv[i]
        pack[c, y] = total
        for i in range(NZ - 1):
            z_copy(t, i).start()

    def after_z(t):
        pack, _, _, zrecv = packs(t)
        for i in range(NZ - 1):
            z_copy(t, i).wait_recv()
        total = pack[c, y, z]
        for i in range(NZ - 1):
            total = total + zrecv[i]
        height = START[t + 1] - START[t]
        b1[START[t] : START[t + 1], :] = total[:height]
        b2[START[t] : START[t + 1], :] = pltpu.roll(total, BLOCK // 2, 1) if t < HALF else total[height:]

    def sent(t):
        for e in PARTNERS:
            x_copy(e, t).wait_send()
        for i in range(NY):
            c_copy(t, i).wait_send()
        for i in range(NY - 1):
            y_copy(t, i).wait_send()
        for i in range(NZ - 1):
            z_copy(t, i).wait_send()

    for t in range(PHASES):
        pair_sums(t)
        if 3 <= t < PHASES - 1:
            after_z(t - 3)
        after_core(t)
        if 3 <= t < PHASES - 1:
            sent(t - 3)
    after_y(PHASES - 3)
    after_z(PHASES - 4)
    after_y(PHASES - 2)
    sent(PHASES - 4)
    after_y(PHASES - 1)
    after_z(PHASES - 3)
    sent(PHASES - 3)
    after_z(PHASES - 2)
    sent(PHASES - 2)
    after_z(PHASES - 1)

    p = lax.broadcasted_iota(jnp.int32, (BLOCK, BLOCK), 0)
    q = lax.broadcasted_iota(jnp.int32, (BLOCK, BLOCK), 1)
    own_end = jnp.where(p < START[FULL], (p // CHUNK + 1) * CHUNK, (p // SUB + 1) * SUB)
    whole = jnp.where(q < own_end, b1[...], b2[...].T)
    fsend[...] = whole.reshape(NOCC, CHUNK, BLOCK)

    def f_copy(e):
        return pltpu.make_async_remote_copy(
            src_ref=fsend.at[occ_to(e)], dst_ref=frecv.at[occ],
            send_sem=fss.at[e], recv_sem=frs.at[e],
            device_id=at_occ(occ_to(e)), device_id_type=MESH,
        )

    for e in PARTNERS:
        f_copy(e).start()
    frecv[occ] = fsend[occ]

    sent(PHASES - 1)
    for e in PARTNERS:
        f_copy(e).wait()
    scale = 1.0 / math.sqrt(AUX * NY * NZ * ORB)
    for parity in range(NC):
        total = frecv[parity]
        for i in range(1, NX):
            total = total + frecv[NC * i + parity]
        out_ref[parity] = total * scale


def shards(three_index, occ_coeff, occ_mask, screen_list, screen_count, owner_order):
    f32, bf16, dma = jnp.float32, jnp.bfloat16, pltpu.SemaphoreType.DMA
    smem = pl.BlockSpec(memory_space=pltpu.SMEM)
    anywhere = pl.BlockSpec(memory_space=pl.ANY)
    return pl.pallas_call(
        kernel,
        out_shape=jax.ShapeDtypeStruct((NC, CHUNK, BLOCK), f32),
        in_specs=[anywhere, anywhere, smem, smem, smem, smem],
        out_specs=pl.BlockSpec(memory_space=pltpu.VMEM),
        scratch_shapes=[
            pltpu.VMEM((CHUNKS, SLOTS, AUX, CHUNK, BLOCK), bf16),
            pltpu.VMEM((NOCC, BLOCK, ORB), bf16),
            pltpu.VMEM((SLOTS * BLOCK, ORB), bf16),
            pltpu.VMEM((len(STEPS), BLOCK, DEPTH), bf16),
            pltpu.VMEM((NOCC, BLOCK, DEPTH), bf16),
            pltpu.VMEM((len(STEPS), 2, CHUNK, DEPTH // 2), bf16),
            pltpu.VMEM((2, NOCC, CHUNK, DEPTH // 2), bf16),
            pltpu.VMEM((CHUNKS // 2, DEPTH, 2 * BLOCK), bf16),
            pltpu.VMEM((2, DEPTH // 2, BLOCK), bf16),
            pltpu.VMEM((CHUNKS, NOCC, CHUNK, BLOCK), f32),
            pltpu.VMEM((NOCC, NOCC, CHUNK, BLOCK), f32),
            *(
                pltpu.VMEM((count, *lead, height, BLOCK), f32)
                for count, height in ((HALF, CHUNK), (FULL - HALF, 2 * CHUNK), (2, CHUNK))
                for lead in ((NC, NY, NZ), (NY, NZ), (NY - 1, NZ), (NZ - 1,))
            ),
            pltpu.VMEM((BLOCK, BLOCK), f32),
            pltpu.VMEM((BLOCK, BLOCK), f32),
            pltpu.VMEM((NOCC, CHUNK, BLOCK), f32),
            pltpu.VMEM((NOCC, CHUNK, BLOCK), f32),
            dma((CHUNKS,)),
            dma((NOCC,)),
            dma,
            dma((len(STEPS), PHASES)),
            dma((len(STEPS), PHASES)),
            dma((PHASES, NY)),
            dma((PHASES, NY)),
            dma((PHASES, NY - 1)),
            dma((PHASES, NY - 1)),
            dma((PHASES, NZ - 1)),
            dma((PHASES, NZ - 1)),
            dma((len(STEPS),)),
            dma((len(STEPS),)),
        ],
        compiler_params=pltpu.CompilerParams(
            collective_id=0, has_side_effects=True, vmem_limit_bytes=56 * 1024 * 1024
        ),
        name="exchange",
    )(three_index, occ_coeff.reshape(NOCC, BLOCK, ORB), occ_mask, screen_list, screen_count, owner_order)


def solution(mesh):
    in_specs = (P("occ", "aux", None, None), P(), P(), P("aux", "occ"), P("aux", "occ"), P())
    out_specs = P("aux", "occ", None)
    return jax.shard_map(shards, mesh=mesh, in_specs=in_specs, out_specs=out_specs, check_vma=False)
```

time: 85.5 us -> 83.9 us (0.981)
  Pallas kernels: 83.3 us -> 81.7 us
    pallas_call x1, Pallas kernels: 83.3 us -> 81.7 us  [shards(): pl.pallas_call(kernel, out_shape=jax.ShapeDtypeStruct((NC, CHUNK, BLOCK),...]
where the time goes in v3:
time: 83.9 us; the launch traced here: 83.7 us
  Pallas kernels  81.7 us (97%)
  local copies, waits for them, and re-layouts  1.32 us (2%)
    pallas_call x1, Pallas kernels, shards(): pl.pallas_call(kernel, out_shape=jax.ShapeDtypeStruct((NC, CHUNK, BLOCK),...  81.7 us

profile of v3, /device:TPU:1, one launch (start us, length us, event | category | flops | bytes accessed | tf_op | source)
XLA Modules:
  0.0 83.7 jit_solution(4038435394983082664)
XLA Ops:
  0.7 81.7 %exchange.1 = f32[2,16,128]{2,1,0:T(8,128)} custom-call(bf16[4,64,128,128]{3,2,1,0:T(8,128)(2,1)} %three_ref.1, bf16[8,128,256]{2,1,0:T(8,128)(2,1)} %bitcast.1, s32[8,8]{1,0:T(8,128)} %mask_ref.1, s32[1,4]{1,0:T(1,128)} %list_ref.1, s32[1,1]{1,0:T(1,128)S(6)} %copy.8.count_ref, s32[64]{0:T(128)} %order_ref.1), custom_call_target="tpu_custom_call" | custom-call | tf_op jit(solution)/shard_map/exchange/pallas_call | solution.py:367
  82.4 1.3 %copy.9 = f32[2,16,128]{2,1,0:T(8,128)} copy(f32[2,16,128]{2,1,0:T(8,128)} %exchange.1) | data formatting | bytes 32768

commit v4 on v3

--- a/solution.py
+++ b/solution.py
@@ -19,6 +19,7 @@
 CHUNKS = BLOCK // CHUNK
 FULL = CHUNKS - 1
 PHASES = FULL + 2
+SPLIT = FULL - 1
 QD = AUX // NOCC
 DEPTH = QD * ORB
 START = (*range(0, BLOCK - CHUNK + 1, CHUNK), BLOCK - SUB, BLOCK)
@@ -32,8 +33,8 @@
 
 def kernel(
     three_ref, coeff_ref, mask_ref, list_ref, count_ref, order_ref, out_ref,
-    tbuf, cbuf, cm, sbuf, xbuf, ssub, xsub, wbuf, wsub, rbuf, hbuf, early, early_c, early_y, early_z, late, late_c, late_y, late_z, last, last_c, last_y, last_z, b1, b2, fsend, frecv,
-    tsem, fsem, csem, xss, xrs, css, crs, yss, yrs, zss, zrs, fss, frs,
+    tbuf, cbuf, cm, sbuf, xbuf, ssub, xsub, wbuf, wsub, rbuf, hbuf, early, early_c, early_y, early_z, late, late_c, late_y, late_z, last, last_c, last_y, last_z, split_y, split_z, b1, b2, fsend, frecv,
+    tsem, fsem, csem, xss, xrs, css, crs, yss, yrs, zss, zrs, szs, szr, sys_, syr, fss, frs,
 ):
     occ, aux = lax.axis_index("occ"), lax.axis_index("aux")
     x, c = occ // NC, occ % NC
@@ -114,18 +115,38 @@
 
     def y_copy(t, i):
         pack, _, yrecv, _ = packs(t)
-        return pltpu.make_async_remote_copy(
-            src_ref=pack.at[c, group_of(i)], dst_ref=yrecv.at[i],
+        source, target = pack.at[c, group_of(i)], yrecv.at[i]
+        if t == SPLIT:
+            source, target = source.at[:, :CHUNK], target.at[:, :CHUNK]
+        return pltpu.make_async_remote_copy(
+            src_ref=source, dst_ref=target,
             send_sem=yss.at[t, i], recv_sem=yrs.at[t, i],
             device_id=at_y(i), device_id_type=MESH,
         )
 
     def z_copy(t, i):
         pack, _, _, zrecv = packs(t)
-        return pltpu.make_async_remote_copy(
-            src_ref=pack.at[c, y, (z + Z_STEPS[i]) % NZ], dst_ref=zrecv.at[i],
+        source, target = pack.at[c, y, (z + Z_STEPS[i]) % NZ], zrecv.at[i]
+        if t == SPLIT:
+            source, target = source.at[:CHUNK], target.at[:CHUNK]
+        return pltpu.make_async_remote_copy(
+            src_ref=source, dst_ref=target,
             send_sem=zss.at[t, i], recv_sem=zrs.at[t, i],
             device_id=at_z(i), device_id_type=MESH,
+        )
+
+    def split_z_copy(i):
+        return pltpu.make_async_remote_copy(
+            src_ref=packs(SPLIT)[0].at[c, :, (z + Z_STEPS[i]) % NZ, CHUNK:], dst_ref=split_z.at[i],
+            send_sem=szs.at[i], recv_sem=szr.at[i],
+            device_id=at_z(i), device_id_type=MESH,
+        )
+
+    def split_y_copy(i):
+        return pltpu.make_async_remote_copy(
+            src_ref=packs(SPLIT)[0].at[c, group_of(i), z, CHUNK:], dst_ref=split_y.at[i],
+            send_sem=sys_.at[i], recv_sem=syr.at[i],
+            device_id=at_y(i), device_id_type=MESH,
         )
 
     def loop(n, body):
@@ -281,28 +302,53 @@
             pack[c, at] = pack[c, at] + crecv[at]
             if i < NY - 1:
                 y_copy(t, i).start()
+        if t == SPLIT:
+            for i in range(NZ - 1):
+                split_z_copy(i).start()
 
     def after_y(t):
         pack, _, yrecv, _ = packs(t)
+        height = CHUNK if t == SPLIT else pack.shape[-2]
         for i in range(NY - 1):
             y_copy(t, i).wait_recv()
-        total = pack[c, y]
-        for i in range(NY - 1):
-            total = total + yrecv[i]
-        pack[c, y] = total
+        total = pack[c, y, :, :height]
+        for i in range(NY - 1):
+            total = total + yrecv[i, :, :height]
+        pack[c, y, :, :height] = total
         for i in range(NZ - 1):
             z_copy(t, i).start()
+
+    def after_split_z():
+        pack = packs(SPLIT)[0]
+        for i in range(NZ - 1):
+            split_z_copy(i).wait_recv()
+        total = pack[c, :, z, CHUNK:]
+        for i in range(NZ - 1):
+            total = total + split_z[i]
+        pack[c, :, z, CHUNK:] = total
+        for i in range(NY - 1):
+            split_y_copy(i).start()
+
+    def after_split_y():
+        for i in range(NY - 1):
+            split_y_copy(i).wait_recv()
+        total = packs(SPLIT)[0][c, y, z, CHUNK:]
+        for i in range(NY - 1):
+            total = total + split_y[i]
+        b2[START[SPLIT] : START[SPLIT + 1], :] = total
 
     def after_z(t):
         pack, _, _, zrecv = packs(t)
+        rows_in = CHUNK if t == SPLIT else pack.shape[-2]
         for i in range(NZ - 1):
             z_copy(t, i).wait_recv()
-        total = pack[c, y, z]
-        for i in range(NZ - 1):
-            total = total + zrecv[i]
+        total = pack[c, y, z, :rows_in]
+        for i in range(NZ - 1):
+            total = total + zrecv[i, :rows_in]
         height = START[t + 1] - START[t]
         b1[START[t] : START[t + 1], :] = total[:height]
-        b2[START[t] : START[t + 1], :] = pltpu.roll(total, BLOCK // 2, 1) if t < HALF else total[height:]
+        if t != SPLIT:
+            b2[START[t] : START[t + 1], :] = pltpu.roll(total, BLOCK // 2, 1) if t < HALF else total[height:]
 
     def sent(t):
         for e in PARTNERS:
@@ -313,6 +359,11 @@
             y_copy(t, i).wait_send()
         for i in range(NZ - 1):
             z_copy(t, i).wait_send()
+        if t == SPLIT:
+            for i in range(NZ - 1):
+                split_z_copy(i).wait_send()
+            for i in range(NY - 1):
+                split_y_copy(i).wait_send()
 
     for t in range(PHASES):
         pair_sums(t)
@@ -326,9 +377,11 @@
     after_y(PHASES - 2)
     sent(PHASES - 4)
     after_y(PHASES - 1)
+    after_split_z()
     after_z(PHASES - 3)
+    after_z(PHASES - 2)
+    after_split_y()
     sent(PHASES - 3)
-    after_z(PHASES - 2)
     sent(PHASES - 2)
     after_z(PHASES - 1)
 
@@ -386,6 +439,8 @@
                 for count, height in ((HALF, CHUNK), (FULL - HALF, 2 * CHUNK), (2, CHUNK))
                 for lead in ((NC, NY, NZ), (NY, NZ), (NY - 1, NZ), (NZ - 1,))
             ),
+            pltpu.VMEM((NY - 1, CHUNK, BLOCK), f32),
+            pltpu.VMEM((NZ - 1, NY, CHUNK, BLOCK), f32),
             pltpu.VMEM((BLOCK, BLOCK), f32),
             pltpu.VMEM((BLOCK, BLOCK), f32),
             pltpu.VMEM((NOCC, CHUNK, BLOCK), f32),
@@ -401,6 +456,10 @@
             dma((PHASES, NY - 1)),
             dma((PHASES, NZ - 1)),
             dma((PHASES, NZ - 1)),
+            dma((NZ - 1,)),
+            dma((NZ - 1,)),
+            dma((NY - 1,)),
+            dma((NY - 1,)),
             dma((len(STEPS),)),
             dma((len(STEPS),)),
         ],

time: 83.9 us -> 83.2 us (level)
  no operation moved by 1% of the time
where the time goes in v4:
time: 83.2 us; the launch traced here: 83 us
  Pallas kernels  81 us (97%)
  local copies, waits for them, and re-layouts  1.32 us (2%)
    pallas_call x1, Pallas kernels, shards(): pl.pallas_call(kernel, out_shape=jax.ShapeDtypeStruct((NC, CHUNK, BLOCK),...  81 us

profile of v4, /device:TPU:1, one launch (start us, length us, event | category | flops | bytes accessed | tf_op | source)
XLA Modules:
  0.0 83.0 jit_solution(7991286483856932029)
XLA Ops:
  0.7 81.0 %exchange.1 = f32[2,16,128]{2,1,0:T(8,128)} custom-call(bf16[4,64,128,128]{3,2,1,0:T(8,128)(2,1)} %three_ref.1, bf16[8,128,256]{2,1,0:T(8,128)(2,1)} %bitcast.1, s32[8,8]{1,0:T(8,128)} %mask_ref.1, s32[1,4]{1,0:T(1,128)} %list_ref.1, s32[1,1]{1,0:T(1,128)S(6)} %copy.8.count_ref, s32[64]{0:T(128)} %order_ref.1), custom_call_target="tpu_custom_call" | custom-call | tf_op jit(solution)/shard_map/exchange/pallas_call | solution.py:420
  81.7 1.3 %copy.9 = f32[2,16,128]{2,1,0:T(8,128)} copy(f32[2,16,128]{2,1,0:T(8,128)} %exchange.1) | data formatting | bytes 32768

commit v5 on v4

--- a/solution.py
+++ b/solution.py
@@ -32,8 +32,8 @@
 
 
 def kernel(
-    three_ref, coeff_ref, mask_ref, list_ref, count_ref, order_ref, out_ref,
-    tbuf, cbuf, cm, sbuf, xbuf, ssub, xsub, wbuf, wsub, rbuf, hbuf, early, early_c, early_y, early_z, late, late_c, late_y, late_z, last, last_c, last_y, last_z, split_y, split_z, b1, b2, fsend, frecv,
+    three_ref, coeff_ref, mask_ref, list_ref, count_ref, order_ref, frecv,
+    tbuf, cbuf, cm, sbuf, xbuf, ssub, xsub, wbuf, wsub, rbuf, hbuf, early, early_c, early_y, early_z, late, late_c, late_y, late_z, last, last_c, last_y, last_z, split_y, split_z, b1, b2, fsend,
     tsem, fsem, csem, xss, xrs, css, crs, yss, yrs, zss, zrs, szs, szr, sys_, syr, fss, frs,
 ):
     occ, aux = lax.axis_index("occ"), lax.axis_index("aux")
@@ -405,11 +405,14 @@
     sent(PHASES - 1)
     for e in PARTNERS:
         f_copy(e).wait()
+
+
+def add_up(parts_ref, out_ref):
     scale = 1.0 / math.sqrt(AUX * NY * NZ * ORB)
     for parity in range(NC):
-        total = frecv[parity]
+        total = parts_ref[parity]
         for i in range(1, NX):
-            total = total + frecv[NC * i + parity]
+            total = total + parts_ref[NC * i + parity]
         out_ref[parity] = total * scale
 
 
@@ -417,9 +420,9 @@
     f32, bf16, dma = jnp.float32, jnp.bfloat16, pltpu.SemaphoreType.DMA
     smem = pl.BlockSpec(memory_space=pltpu.SMEM)
     anywhere = pl.BlockSpec(memory_space=pl.ANY)
-    return pl.pallas_call(
+    parts = pl.pallas_call(
         kernel,
-        out_shape=jax.ShapeDtypeStruct((NC, CHUNK, BLOCK), f32),
+        out_shape=jax.ShapeDtypeStruct((NOCC, CHUNK, BLOCK), f32),
         in_specs=[anywhere, anywhere, smem, smem, smem, smem],
         out_specs=pl.BlockSpec(memory_space=pltpu.VMEM),
         scratch_shapes=[
@@ -444,7 +447,6 @@
             pltpu.VMEM((BLOCK, BLOCK), f32),
             pltpu.VMEM((BLOCK, BLOCK), f32),
             pltpu.VMEM((NOCC, CHUNK, BLOCK), f32),
-            pltpu.VMEM((NOCC, CHUNK, BLOCK), f32),
             dma((CHUNKS,)),
             dma((NOCC,)),
             dma,
@@ -468,6 +470,13 @@
         ),
         name="exchange",
     )(three_index, occ_coeff.reshape(NOCC, BLOCK, ORB), occ_mask, screen_list, screen_count, owner_order)
+    return pl.pallas_call(
+        add_up,
+        out_shape=jax.ShapeDtypeStruct((NC, CHUNK, BLOCK), f32),
+        in_specs=[pl.BlockSpec(memory_space=pltpu.VMEM)],
+        out_specs=pl.BlockSpec(memory_space=pltpu.VMEM),
+        name="add_up",
+    )(parts)
 
 
 def solution(mesh):

time: 83.2 us -> 83.4 us (level)
  Pallas kernels: 81 us -> 82.5 us
  local copies, waits for them, and re-layouts: 1.32 us -> 0 us
    pallas_call x1 -> x2, Pallas kernels: 81 us -> 82.5 us  [the longest x1 81.1 us: shards(): pl.pallas_call(kernel, out_shape=jax.ShapeDtypeStruct((NOCC, CHUNK, BLOCK...]
    unnamed x1 -> x0, local copies, waits for them, and re-layouts: 1.32 us -> none
where the time goes in v5:
time: 83.4 us; the launch traced here: 83.2 us
  Pallas kernels  82.5 us (99%)
    pallas_call x1, Pallas kernels, shards(): pl.pallas_call(kernel, out_shape=jax.ShapeDtypeStruct((NOCC, CHUNK, BLOCK...  81.1 us

profile of v5, /device:TPU:1, one launch (start us, length us, event | category | flops | bytes accessed | tf_op | source)
XLA Modules:
  0.0 83.2 jit_solution(975579620857102191)
XLA Ops:
  0.7 81.1 %exchange.1.parts_ref = f32[8,16,128]{2,1,0:T(8,128)} custom-call(bf16[4,64,128,128]{3,2,1,0:T(8,128)(2,1)} %three_ref.1, bf16[8,128,256]{2,1,0:T(8,128)(2,1)} %bitcast.1, s32[8,8]{1,0:T(8,128)} %mask_ref.1, s32[1,4]{1,0:T(1,128)} %list_ref.1, s32[1,1]{1,0:T(1,128)S(6)} %copy.7.count_ref, s32[64]{0:T(128)} %order_ref.1), custom_call_target="tpu_custom_call" | custom-call | tf_op jit(solution)/shard_map/exchange/pallas_call | solution.py:423
  81.7 1.5 %add_up.1 = f32[2,16,128]{2,1,0:T(8,128)} custom-call(f32[8,16,128]{2,1,0:T(8,128)} %exchange.1.parts_ref), custom_call_target="tpu_custom_call" | custom-call | tf_op jit(solution)/shard_map/add_up/pallas_call | solution.py:473
